TPU v7x, 32 devices: a whole 2x2x4 slice. The times are simulated.
32 devices in a mesh: parts: 1, row: 8 (over z, y), col: 1, depth: 4 (over x, core).
Axes of the slice: x: 2, y: 2, z: 4, core: 2. Of those that a mesh axis runs over, the one named last changes fastest.
Arguments:
- activations: bfloat16 [4, 256, 8192], P(('parts', 'depth'), 'row', 'col'), may hold values from -6 to 6
- hidden_grads: bfloat16 [4, 256, 16384], P(('parts', 'depth'), 'col', 'row'), may hold values from -0.1875 to 0.1875
Outputs:
- weight_grad: bfloat16 [8192, 16384], P(('parts', 'col', 'depth'), 'row')
All inputs are finite; a program needn't handle non-finite values.
Results may differ from a plain program's by a relative error of at most 0.013.
Values may be sent and summed in bfloat16 or wider, within the bound.
A program may use at most 128 MiB of HBM per device.

v0:
```python
import jax
import jax.numpy as jnp
from jax import lax
from jax.sharding import PartitionSpec as P


def local(activations, hidden_grads):
    swapped = lax.all_to_all(activations, "depth", split_axis=2, concat_axis=0, tiled=True)
    acts = lax.all_gather(swapped, "row", axis=1, tiled=True)
    grads = lax.all_gather(hidden_grads, "depth", axis=0, tiled=True)
    grads = lax.all_gather(grads, "col", axis=1, tiled=True)
    total = lax.dot_general(
        acts, grads, (((0, 1), (0, 1)), ((), ())), preferred_element_type=jnp.float32
    )
    return total.astype(jnp.bfloat16)


def solution(mesh):
    in_specs = (P(("parts", "depth"), "row", "col"), P(("parts", "depth"), "col", "row"))
    out_specs = P(("parts", "col", "depth"), "row")
    return jax.shard_map(local, mesh=mesh, in_specs=in_specs, out_specs=out_specs, check_vma=False)
```

profile of v0, /device:TPU:0, one launch (start us, length us, event | category | flops | bytes accessed | tf_op | source)
XLA Modules:
  0.0 217.2 jit_solution(3695399159835913625)
XLA Ops:
  6.5 0.0 all-gather.6.cloned.1.call-start
  6.5 8.6 %copy.7 = bf16[1,32,8192]{1,0,2:T(2,128)(2,1)} copy(bf16[1,32,8192]{2,1,0:T(8,128)(2,1)} %param.2) | data formatting | bytes 1048576 | tf_op args[0]
  15.1 0.5 broadcast
  15.6 45.2 %reduce = bf16[8192,32]{1,0:T(8,128)(2,1)S(1)} reduce(bf16[8192,1,32]{2,1,0:T(2,128)(2,1)} %bitcast.11, bf16[]{:T(256)} %broadcast), dimensions={1}, to_apply=%bitcast.8.reduce_sub_computation | reduce | bytes 1048578
  60.8 2.2 reshape.2
  63.0 12.9 %all_to_all.18 = bf16[4,2,32768]{2,1,0:T(2,128)(2,1)S(1)} all-to-all(bf16[4,2,32768]{2,1,0:T(2,128)(2,1)S(1)} %reshape.2), channel_id=1, replica_groups=mesh['parts'=1,'row'=8,'col'=1,'depth'=4] {'depth'}, dimensions={0} | all-to-all | bytes 1048576 | tf_op jit(solution)/shard_map/all_to_all | solution.py:8
  75.9 3.3 %reshape.3 = bf16[8192,1,32]{2,1,0:T(2,128)(2,1)} reshape(bf16[4,2,32768]{2,1,0:T(2,128)(2,1)S(1)} %all_to_all.18) | data formatting | bytes 1048576
  79.1 8.0 %copy.8 = bf16[1,32,8192]{2,1,0:T(8,128)(2,1)S(1)} copy(bf16[1,32,8192]{1,0,2:T(2,128)(2,1)} %bitcast.12) | data formatting | bytes 1048576 | tf_op jit(solution)/shard_map/all_to_all | solution.py:8
  87.1 1.2 all_to_all.14
  88.3 0.0 all-gather.6.cloned.1.call-update
  88.3 0.2 all-gather.4.cloned.1.call-start
  88.5 0.5 all-gather.4.cloned.1.call-update
  89.0 73.1 %all-gather.6.cloned.1.call-done = bf16[4,1,256,2048]{3,0,1,2:T(4,128)(2,1)} async-done(((bf16[4,1,32,2048]{3,0,1,2:T(4,128)(2,1)}), bf16[4,1,256,2048]{3,0,1,2:T(4,128)(2,1)}) %all-gather.6.cloned.1.call-update) | async-done | bytes 4194320 | tf_op jit(solution)/shard_map/all_gather | solution.py:9
  162.2 7.6 %copy.10 = bf16[4,1,256,2048]{2,3,0,1:T(8,128)(2,1)} copy(bf16[4,1,256,2048]{3,0,1,2:T(4,128)(2,1)} %all-gather.6.cloned.1.call-done) | data formatting | bytes 8388608 | tf_op jit(solution)/shard_map/all_gather | solution.py:9
  169.7 26.8 %all-gather.4.cloned.1.call-done = bf16[4,256,2048]{2,1,0:T(8,128)(2,1)} async-done(((bf16[1,256,2048]{2,1,0:T(8,128)(2,1)}), bf16[4,256,2048]{2,1,0:T(8,128)(2,1)}) %all-gather.4.cloned.1.call-update) | async-done | bytes 4194320 | tf_op jit(solution)/shard_map/all_gather | solution.py:10
  196.5 13.9 %bitcast_convert_fusion = bf16[2048,2048]{1,0:T(8,128)(2,1)} fusion(bf16[4,256,2048]{2,1,0:T(8,128)(2,1)} %all-gather.4.cloned.1.call-done, bf16[4,1,256,2048]{2,3,0,1:T(8,128)(2,1)} %copy.10), kind=kOutput, calls=%fused_computation | convolution fusion | flops 8594128896 | bytes 16777216 | tf_op jit(solution)/shard_map/dot_general | solution.py:12
Async XLA Ops:
  6.5 155.6 %all-gather.6.cloned.1.call-start = ((), (), s32[]{:S(2)}) async-start(), calls=%async_computation.2 | async-start | bytes 4718592 | tf_op jit(solution)/shard_map/all_gather | solution.py:9
  88.3 108.2 %all-gather.4.cloned.1.call-start = ((), (), s32[]{:S(2)}) async-start(), calls=%async_computation.1 | async-start | bytes 5242880 | tf_op jit(solution)/shard_map/all_gather | solution.py:10
Sparse Core Ops, SparseCore 0:
  88.4 73.7 all-gather.5
  163.7 32.7 all-gather.3
where the time goes:
time: 218 us; the launch traced here: 217 us
  waiting for transfers between devices  100 us (46%)
  other arithmetic  45.2 us (21%)
  local copies, waits for them, and re-layouts  31.2 us (14%)
  matrix products  13.9 us (6%)
  between operations  13.4 us (6%)
  blocking collectives  12.9 us (6%)
    all_gather x1, waiting for transfers between devices, local(): acts = lax.all_gather(swapped, 'row', axis=1, tiled=True)  73.1 us
    unnamed x1, other arithmetic  45.2 us
    all_gather x1, waiting for transfers between devices, local(): grads = lax.all_gather(hidden_grads, 'depth', axis=0, tiled=True)  26.8 us
    unnamed x4, local copies, waits for them, and re-layouts  14.5 us
    dot_general x1, matrix products, local(): lax.dot_general(acts, grads, (((0, 1), (0, 1)), ((), ())), preferred_elem...  13.9 us
    all_to_all x1, blocking collectives, local(): lax.all_to_all(activations, 'depth', split_axis=2, concat_axis=0, tiled=T...  12.9 us
    all_to_all x2, local copies, waits for them, and re-layouts, local(): lax.all_to_all(activations, 'depth', split_axis=2, concat_axis=0, tiled=T...  9.14 us
    all_gather x1, local copies, waits for them, and re-layouts, local(): acts = lax.all_gather(swapped, 'row', axis=1, tiled=True)  7.56 us
  transfers between devices with their start and end apart: 2, of which 2 were waited for; matrix products, arithmetic and copies ran while one was open for 3% of the time, Pallas kernels for 0%

commit v1 on v0

--- a/solution.py
+++ b/solution.py
@@ -1,11 +1,44 @@
+import functools
 import jax
 import jax.numpy as jnp
 from jax import lax
 from jax.sharding import PartitionSpec as P
 
 
+def pass_quarters(field, d0, target):
+    k_now, all_rows = (field.shape[:d0], field.shape[d0 + 1 :])
+    return jnp.moveaxis(field.reshape(*k_now, target, -1, *all_rows), d0, 0)
+
+
+def _meet_links(m, dim_no):
+    m = jnp.moveaxis(m, 0, dim_no)
+    moved = m.shape
+    return m.reshape(*moved[:dim_no], moved[dim_no] * moved[dim_no + 1], *moved[dim_no + 2 :])
+
+
+def point_scenes(v0, along_axis, z_in, shard_in):
+    local_next = lax.axis_size(along_axis)
+    arr_next = lax.axis_index(along_axis)
+    reply, u1 = (local_next, arr_next)
+    q_next = pass_quarters(v0, z_in, reply)
+    v1 = q_next
+    for i0 in range(1, reply):
+        step_out, finding = ((u1 + i0) % reply, (u1 - i0) % reply)
+        later = lax.dynamic_index_in_dim(q_next, step_out, 0)
+        r1 = lax.ppermute(
+            later,
+            along_axis,
+            list(map(lambda hop_no: (hop_no, (hop_no + i0) % reply), range(reply))),
+        )
+        v1 = lax.dynamic_update_slice_in_dim(v1, r1, finding, axis=0)
+    return _meet_links(v1, shard_in)
+
+
+_lift_pairs_all = functools.partial(point_scenes, along_axis="depth", z_in=2, shard_in=0)
+
+
 def local(activations, hidden_grads):
-    swapped = lax.all_to_all(activations, "depth", split_axis=2, concat_axis=0, tiled=True)
+    swapped = _lift_pairs_all(activations)
     acts = lax.all_gather(swapped, "row", axis=1, tiled=True)
     grads = lax.all_gather(hidden_grads, "depth", axis=0, tiled=True)
     grads = lax.all_gather(grads, "col", axis=1, tiled=True)

time: 218 us -> 143 us (0.66)
  other arithmetic: 45.2 us -> 0 us
  local copies, waits for them, and re-layouts: 31.2 us -> 3.36 us
  blocking collectives: 12.9 us -> 0 us
  waiting for transfers between devices: 100 us -> 107 us
  starting transfers between devices: 0.22 us -> 4.61 us
    unnamed x1 -> x0, other arithmetic: 45.2 us -> none
    unnamed x4 -> x7, local copies, waits for them, and re-layouts: 14.5 us -> 1.04 us
    all_to_all x1 -> x0, blocking collectives: 12.9 us -> none  [local(): lax.all_to_all(activations, 'depth', split_axis=2, concat_axis=0, tiled=T...]
    all_to_all x2 -> x0, local copies, waits for them, and re-layouts: 9.14 us -> none  [local(): lax.all_to_all(activations, 'depth', split_axis=2, concat_axis=0, tiled=T...]
    all_gather x1 -> x0, local copies, waits for them, and re-layouts: 7.56 us -> none  [local(): acts = lax.all_gather(swapped, 'row', axis=1, tiled=True)]
    ppermute x0 -> x3, starting transfers between devices: none -> 4.57 us  [point_scenes(): lax.ppermute(later, along_axis, list(map(lambda hop_no: (hop_no, (hop_no...]
    ppermute x0 -> x3, waiting for transfers between devices: none -> 4.29 us  [point_scenes(): lax.ppermute(later, along_axis, list(map(lambda hop_no: (hop_no, (hop_no...]
    all_gather x1, waiting for transfers between devices: 73.1 us -> 75.6 us  [local(): acts = lax.all_gather(swapped, 'row', axis=1, tiled=True)]
  transfers between devices with their start and end apart: 2 -> 5, of which waited for: 2 -> 5; matrix products, arithmetic and copies ran while one was open for 3% -> 2% of each run, Pallas kernels for 0% -> 0%
where the time goes in v1:
time: 143 us
  waiting for transfers between devices  107 us (75%)
  matrix products  14 us (10%)
  between operations  13.5 us (9%)
  starting transfers between devices  4.61 us (3%)
  local copies, waits for them, and re-layouts  3.36 us (2%)
    all_gather x1, waiting for transfers between devices, local(): acts = lax.all_gather(swapped, 'row', axis=1, tiled=True)  75.6 us
    all_gather x1, waiting for transfers between devices, local(): grads = lax.all_gather(hidden_grads, 'depth', axis=0, tiled=True)  26.5 us
    dot_general x1, matrix products, local(): lax.dot_general(acts, grads, (((0, 1), (0, 1)), ((), ())), preferred_elem...  14 us
    ppermute x3, starting transfers between devices, point_scenes(): lax.ppermute(later, along_axis, list(map(lambda hop_no: (hop_no, (hop_no...  4.57 us
    ppermute x3, waiting for transfers between devices, point_scenes(): lax.ppermute(later, along_axis, list(map(lambda hop_no: (hop_no, (hop_no...  4.29 us
  transfers between devices with their start and end apart: 5, of which 5 were waited for; matrix products, arithmetic and copies ran while one was open for 2% of the time, Pallas kernels for 0%

profile of v1, /device:TPU:0, one launch (start us, length us, event | category | flops | bytes accessed | tf_op | source)
XLA Modules:
  0.0 142.6 jit_solution(15523267363646797287)
XLA Ops:
  6.5 0.0 copy-start
  6.5 0.0 all-gather.5.cloned.1.call-start
  6.5 0.7 all-gather.5.cloned.1.call-update
  7.3 0.0 all-gather.3.cloned.1.call-start
  7.3 1.4 %reshape.21 = bf16[1,32,4,2048]{3,2,1,0:T(4,128)(2,1)S(1)} reshape(bf16[1,32,8192]{2,1,0:T(8,128)(2,1)} %param.2) | data formatting | bytes 1048576 | tf_op jit(solution)/shard_map/reshape | solution.py:10
  8.8 0.8 constant_dynamic-slice_fusion
  9.6 0.1 copy.17
  9.7 0.5 collective-permute-start
  10.2 0.1 copy.16
  10.3 2.6 %collective-permute-start.1 = (bf16[1,1,32,2048]{3,2,1,0:T(8,128)(2,1)S(1)}, bf16[1,1,32,2048]{3,2,1,0:T(8,128)(2,1)S(1)}, u32[]{:S(2)}, u32[]{:S(2)}) collective-permute-start(bf16[1,1,32,2048]{3,2,1,0:T(8,128)(2,1)S(1)} %bitcast.31), channel_id=1, source_target_pairs={{0,2},{1,3},{2,0},{3,1},{4,6},{5,7},{6,4},{7,5},{8,10},{9,11},{10,... | collective-permute-start | bytes 393224 | tf_op jit(solution)/shard_map/ppermute | solution.py:28
  12.9 0.1 copy.15
  12.9 1.5 %collective-permute-start.2 = (bf16[1,1,32,2048]{3,2,1,0:T(8,128)(2,1)S(1)}, bf16[1,1,32,2048]{3,2,1,0:T(8,128)(2,1)S(1)}, u32[]{:S(2)}, u32[]{:S(2)}) collective-permute-start(bf16[1,1,32,2048]{3,2,1,0:T(8,128)(2,1)S(1)} %bitcast.30), channel_id=1, source_target_pairs={{0,3},{1,0},{2,1},{3,2},{4,7},{5,4},{6,5},{7,6},{8,11},{9,8},{10,9... | collective-permute-start | bytes 393224 | tf_op jit(solution)/shard_map/ppermute | solution.py:28
  14.4 0.0 copy-done
  14.5 0.7 collective-permute-done
  15.2 1.6 %collective-permute-done.1 = bf16[1,1,32,2048]{3,2,1,0:T(8,128)(2,1)S(1)} collective-permute-done((bf16[1,1,32,2048]{3,2,1,0:T(8,128)(2,1)S(1)}, bf16[1,1,32,2048]{3,2,1,0:T(8,128)(2,1)S(1)}, u32[]{:S(2)}, u32[]{:S(2)}) %collective-permute-start.1) | collective-permute-done | bytes 131104 | tf_op jit(solution)/shard_map/ppermute | solution.py:28
  16.8 2.0 %collective-permute-done.2 = bf16[1,1,32,2048]{3,2,1,0:T(8,128)(2,1)S(1)} collective-permute-done((bf16[1,1,32,2048]{3,2,1,0:T(8,128)(2,1)S(1)}, bf16[1,1,32,2048]{3,2,1,0:T(8,128)(2,1)S(1)}, u32[]{:S(2)}, u32[]{:S(2)}) %collective-permute-start.2) | collective-permute-done | bytes 131104 | tf_op jit(solution)/shard_map/ppermute | solution.py:28
  18.8 0.0 copy-start.1
  18.9 0.8 copy-done.1
  19.6 0.0 all-gather.3.cloned.1.call-update
  19.7 26.5 %all-gather.5.cloned.1.call-done = bf16[4,256,2048]{2,1,0:T(8,128)(2,1)} async-done(((bf16[1,256,2048]{2,1,0:T(8,128)(2,1)}), bf16[4,256,2048]{2,1,0:T(8,128)(2,1)}) %all-gather.5.cloned.1.call-update) | async-done | bytes 4194320 | tf_op jit(solution)/shard_map/all_gather | solution.py:43
  46.1 75.6 %all-gather.3.cloned.1.call-done = bf16[4,256,2048]{2,1,0:T(8,128)(2,1)} async-done(((bf16[4,32,2048]{2,1,0:T(8,128)(2,1)}), bf16[4,256,2048]{2,1,0:T(8,128)(2,1)}) %all-gather.3.cloned.1.call-update) | async-done | bytes 4194320 | tf_op jit(solution)/shard_map/all_gather | solution.py:42
  121.7 14.0 %bitcast_convert_fusion = bf16[2048,2048]{1,0:T(8,128)(2,1)} fusion(bf16[4,256,2048]{2,1,0:T(8,128)(2,1)} %all-gather.3.cloned.1.call-done, bf16[4,256,2048]{2,1,0:T(8,128)(2,1)} %all-gather.5.cloned.1.call-done), kind=kOutput, calls=%fused_computation | convolution fusion | flops 8594128896 | bytes 16777216 | tf_op jit(solution)/shard_map/dot_general | solution.py:45
  (4 shorter events, 0.1 us)
Async XLA Ops:
  6.5 7.9 %copy-start = (bf16[1,32,8192]{2,1,0:T(8,128)(2,1)S(1)}, bf16[1,32,8192]{2,1,0:T(8,128)(2,1)}, u32[]{:S(2)}) copy-start(bf16[1,32,8192]{2,1,0:T(8,128)(2,1)} %param.2) | copy-start | bytes 1572868
  6.5 39.6 %all-gather.5.cloned.1.call-start = ((), (), s32[]{:S(2)}) async-start(), calls=%async_computation.1 | async-start | bytes 5242880 | tf_op jit(solution)/shard_map/all_gather | solution.py:43
  7.3 114.5 %all-gather.3.cloned.1.call-start = ((), (), s32[]{:S(2)}) async-start(), calls=%async_computation | async-start | bytes 4718592 | tf_op jit(solution)/shard_map/all_gather | solution.py:42
  9.7 5.5 %collective-permute-start = (bf16[1,1,32,2048]{3,2,1,0:T(8,128)(2,1)S(1)}, bf16[1,1,32,2048]{3,2,1,0:T(8,128)(2,1)S(1)}, u32[]{:S(2)}, u32[]{:S(2)}) collective-permute-start(bf16[1,1,32,2048]{3,2,1,0:T(8,128)(2,1)S(1)} %bitcast.32), channel_id=1, source_target_pairs={{0,1},{1,2},{2,3},{3,0},{4,5},{5,6},{6,7},{7,4},{8,9},{9,10},{10,1... | collective-permute-start | bytes 393224 | tf_op jit(solution)/shard_map/ppermute | solution.py:28
  10.3 6.5 %collective-permute-start.1 = (bf16[1,1,32,2048]{3,2,1,0:T(8,128)(2,1)S(1)}, bf16[1,1,32,2048]{3,2,1,0:T(8,128)(2,1)S(1)}, u32[]{:S(2)}, u32[]{:S(2)}) collective-permute-start(bf16[1,1,32,2048]{3,2,1,0:T(8,128)(2,1)S(1)} %bitcast.31), channel_id=1, source_target_pairs={{0,2},{1,3},{2,0},{3,1},{4,6},{5,7},{6,4},{7,5},{8,10},{9,11},{10,... | collective-permute-start | bytes 393224 | tf_op jit(solution)/shard_map/ppermute | solution.py:28
  12.9 5.9 %collective-permute-start.2 = (bf16[1,1,32,2048]{3,2,1,0:T(8,128)(2,1)S(1)}, bf16[1,1,32,2048]{3,2,1,0:T(8,128)(2,1)S(1)}, u32[]{:S(2)}, u32[]{:S(2)}) collective-permute-start(bf16[1,1,32,2048]{3,2,1,0:T(8,128)(2,1)S(1)} %bitcast.30), channel_id=1, source_target_pairs={{0,3},{1,0},{2,1},{3,2},{4,7},{5,4},{6,5},{7,6},{8,11},{9,8},{10,9... | collective-permute-start | bytes 393224 | tf_op jit(solution)/shard_map/ppermute | solution.py:28
  18.8 0.8 copy-start.1
Sparse Core Ops, SparseCore 0:
  8.9 37.1 all-gather.4
  48.3 73.3 all-gather.2
